TPU v7x, 768 devices: a whole 4x8x12 slice. The times are simulated.
768 devices in a mesh: sub: 24 (over y_lo, z), blk: 32 (over y_hi, x, core).
Axes of the slice: x: 4, y: 8 (y_hi: 4, y_lo: 2; y = y_hi * 2 + y_lo), z: 12, core: 2. Of those that a mesh axis runs over, the one named last changes fastest.
Arguments:
- inv_factor: bfloat16 [768, 512, 512], P(('sub', 'blk')), may hold values from -0.25 to 0.25
- coupling: bfloat16 [768, 8, 512, 256], P(('sub', 'blk')), may hold values from -0.25 to 0.25
- batch_coupling: bfloat16 [768, 1, 16, 512], P(('sub', 'blk')), may hold values from -6 to 6
- tile_rows: int32 [768, 8], P(('sub', 'blk')), may hold values from 0 to 1535, as said below
- tile_count: int32 [768], P(('sub', 'blk')), may hold values from 6 to 8, as said below
- row_place: int32 [1536], replicated, may hold values from 0 to 1535, as said below
Outputs:
- schur_update: float32 [1536, 1, 16, 256], P(('sub', 'blk'))
Inputs may be any that keep to these rules, and one draw needn't show every extreme that they name: `tile_rows`: the tiles of one group name distinct rows. With place = row_place[row], owner = place // 64 and block = (place % 64) // 2: at most 2 tiles of one group have one owner, at most 2 live tiles of all groups of one blk index have one owner and one block, and in every draw both bounds are reached. `tile_count`: padding tiles hold arbitrary values. `row_place`: A permutation of the block rows.
All inputs are finite; a program needn't handle non-finite values.
Results may differ from a plain program's by a relative error of at most 0.013.
Values may be sent and summed in bfloat16 or wider, within the bound.
A program may use at most 32 MiB of HBM per device.

v0:
```python
import jax
import jax.numpy as jnp
from jax import lax
from jax.sharding import PartitionSpec as P


def block_products(factor, tiles_in, flat_columns):
    projected = lax.dot_general(
        flat_columns, factor, (((1,), (1,)), ((), ())), preferred_element_type=jnp.float32
    ).astype(jnp.bfloat16)
    solved = jnp.dot(projected, factor, preferred_element_type=jnp.float32).astype(jnp.bfloat16)
    return jnp.einsum("cn,tnf->tcf", solved, tiles_in, preferred_element_type=jnp.float32).astype(
        jnp.bfloat16
    )


def slot_layout(dest, valid, rows_value, targets, capacity):
    num_items = dest.shape[0]
    positions = jnp.arange(num_items, dtype=jnp.int32)
    earlier = (
        (dest[:, None] == dest[None, :])
        & valid[None, :]
        & (positions[None, :] < positions[:, None])
    )
    rank = jnp.sum(earlier.astype(jnp.int32), axis=1)
    slot = jnp.where(valid, dest * capacity + rank, -1)
    slot_hits = jnp.arange(targets * capacity, dtype=jnp.int32)[:, None] == slot[None, :]
    filled = jnp.any(slot_hits, axis=1)
    slot_rows = jnp.where(filled, jnp.sum(jnp.where(slot_hits, rows_value[None, :], 0), axis=1), -1)
    return (slot_hits.astype(jnp.bfloat16), slot_rows.reshape(targets, capacity))


def row_terms(flat_tiles, flat_rows, count_rows):
    wanted = jnp.arange(count_rows, dtype=jnp.int32)
    pick = (wanted[:, None] == flat_rows[None, :]).astype(jnp.bfloat16)
    return jnp.dot(pick, flat_tiles, preferred_element_type=jnp.float32)


def on_device(inv_factor, coupling, batch_coupling, tile_rows, tile_count, row_place):
    factor = inv_factor[0]
    tiles_in = coupling[0]
    columns = batch_coupling[0]
    tile_ids = tile_rows[0]
    count = tile_count[0]
    groups = lax.axis_size("sub")
    owners_blk = lax.axis_size("blk")
    num_rows = row_place.shape[0]
    rows_owned = num_rows // groups
    rows_here = rows_owned // owners_blk
    num_tiles = tiles_in.shape[0]
    capacity = max(2, (num_tiles + groups - 1) // groups)
    batches, width_cols, interior = columns.shape
    block_width = tiles_in.shape[2]
    all_rows = jnp.arange(num_rows, dtype=jnp.int32)
    placed = jnp.sum(
        jnp.where(all_rows[None, :] == tile_ids[:, None], row_place[None, :], 0), axis=1
    )
    target = placed // rows_owned
    local_row = placed % rows_owned
    live = jnp.arange(num_tiles, dtype=jnp.int32) < count
    select, slot_rows = slot_layout(target, live, local_row, groups, capacity)
    partial_value = block_products(
        factor, tiles_in, columns.reshape(batches * width_cols, interior)
    )
    flat_part = partial_value.reshape(num_tiles, batches * width_cols * block_width)
    packed = jnp.dot(select, flat_part, preferred_element_type=jnp.float32).astype(jnp.bfloat16)
    packed = packed.reshape(groups, capacity, flat_part.shape[1])
    got_tiles, got_rows = (
        lax.all_to_all(packed, "sub", split_axis=0, concat_axis=0, tiled=True),
        lax.all_to_all(slot_rows, "sub", split_axis=0, concat_axis=0, tiled=True),
    )
    flat_tiles = got_tiles.reshape(groups * capacity, got_tiles.shape[2])
    flat_rows = got_rows.reshape(groups * capacity)
    summed = lax.psum_scatter(
        row_terms(flat_tiles, flat_rows, rows_here * lax.axis_size("blk")).astype(jnp.bfloat16),
        "blk",
        scatter_dimension=0,
        tiled=True,
    ).astype(jnp.float32)
    return -summed.reshape(rows_here, batches, width_cols, block_width)


def solution(mesh):
    return jax.shard_map(
        on_device,
        mesh=mesh,
        in_specs=(
            P(("sub", "blk"), None, None),
            P(("sub", "blk"), None, None, None),
            P(("sub", "blk"), None, None, None),
            P(("sub", "blk"), None),
            P(("sub", "blk")),
            P(),
        ),
        out_specs=P(("sub", "blk"), None, None, None),
        check_vma=False,
    )
```

profile of v0, /device:TPU:1, one launch (start us, length us, event | category | flops | bytes accessed | tf_op | source)
XLA Modules:
  0.0 360.4 jit_solution(6413040480894160075)
XLA Ops:
  6.5 0.0 copy-start
  6.5 1.0 select_reduce_fusion
  8.3 0.2 convert_reduce_fusion
  8.4 0.1 fusion.14
  8.5 0.1 select_reduce_fusion.1
  8.6 0.7 select_n.64
  9.3 16.9 %all-to-all-start = ((s32[24,1,2]{2,1,0:T(1,128)}), s32[24,1,2]{2,1,0:T(1,128)S(1)}, u32[]{:S(2)}, u32[]{:S(2)}) async-start(s32[24,1,2]{2,1,0:T(1,128)} %bitcast.2), calls=%async_computation | async-start | bytes 24576 | tf_op jit(solution)/shard_map/all_to_all | solution.py:70
  26.3 1.6 fusion.8
  27.9 0.0 copy-done
  27.9 0.4 fusion.5
  28.3 0.4 convolution_convert_fusion.1
  28.7 1.0 reshape.112
  29.7 6.1 %all-to-all-done = s32[24,1,2]{2,1,0:T(1,128)S(1)} async-done(((s32[24,1,2]{2,1,0:T(1,128)}), s32[24,1,2]{2,1,0:T(1,128)S(1)}, u32[]{:S(2)}, u32[]{:S(2)}) %all-to-all-start) | async-done | bytes 224 | tf_op jit(solution)/shard_map/all_to_all | solution.py:70
  35.8 3.9 %all-to-all-start.1 = ((bf16[24,2,4096]{2,1,0:T(2,128)(2,1)}), bf16[24,2,4096]{2,1,0:T(2,128)(2,1)S(1)}, u32[]{:S(2)}, u32[]{:S(2)}) async-start(bf16[24,2,4096]{2,1,0:T(2,128)(2,1)} %reshape.112), calls=%async_computation.1 | async-start | bytes 786432 | tf_op jit(solution)/shard_map/all_to_all | solution.py:69
  39.7 0.0 all-reduce.3.cloned.1.call-start
  39.8 0.5 broadcast.150
  40.3 0.7 reduce.3
  41.0 0.1 eq.69
  41.1 14.9 %all-to-all-done.1 = bf16[24,2,4096]{2,1,0:T(2,128)(2,1)S(1)} async-done(((bf16[24,2,4096]{2,1,0:T(2,128)(2,1)}), bf16[24,2,4096]{2,1,0:T(2,128)(2,1)S(1)}, u32[]{:S(2)}, u32[]{:S(2)}) %all-to-all-start.1) | async-done | bytes 393248 | tf_op jit(solution)/shard_map/all_to_all | solution.py:69
  56.0 0.1 reshape.113
  56.2 1.1 convolution_convert_fusion
  57.3 0.0 all-reduce.3.cloned.1.call-update
  57.3 1.3 dynamic-slice
  59.2 292.9 %all-reduce.3.cloned.1.call-done = bf16[64,4096]{1,0:T(8,128)(2,1)} async-done(((bf16[64,4096]{1,0:T(8,128)(2,1)}), bf16[64,4096]{1,0:T(8,128)(2,1)}) %all-reduce.3.cloned.1.call-update) | async-done | bytes 524304
  352.1 0.9 convert_negate_fusion
  353.0 0.6 copy.16
  (5 shorter events, 0.1 us)
Async XLA Ops:
  6.5 21.3 %copy-start = (bf16[1,8,512,256]{3,2,1,0:T(8,128)(2,1)S(1)}, bf16[1,8,512,256]{3,2,1,0:T(8,128)(2,1)}, u32[]{:S(2)}) copy-start(bf16[1,8,512,256]{3,2,1,0:T(8,128)(2,1)} %param.7) | copy-start | bytes 6291460
  9.3 26.5 %all-to-all-start = ((s32[24,1,2]{2,1,0:T(1,128)}), s32[24,1,2]{2,1,0:T(1,128)S(1)}, u32[]{:S(2)}, u32[]{:S(2)}) async-start(s32[24,1,2]{2,1,0:T(1,128)} %bitcast.2), calls=%async_computation | async-start | bytes 24576 | tf_op jit(solution)/shard_map/all_to_all | solution.py:70
  35.8 20.2 %all-to-all-start.1 = ((bf16[24,2,4096]{2,1,0:T(2,128)(2,1)}), bf16[24,2,4096]{2,1,0:T(2,128)(2,1)S(1)}, u32[]{:S(2)}, u32[]{:S(2)}) async-start(bf16[24,2,4096]{2,1,0:T(2,128)(2,1)} %reshape.112), calls=%async_computation.1 | async-start | bytes 786432 | tf_op jit(solution)/shard_map/all_to_all | solution.py:69
  39.7 312.4 %all-reduce.3.cloned.1.call-start = ((), (), s32[]{:S(2)}) async-start(), calls=%async_computation.2 | async-start | bytes 1048576
Sparse Core Ops, SparseCore 0:
  57.4 294.6 all-reduce.2
where the time goes:
time: 361 us; the launch traced here: 360 us
  waiting for transfers between devices  314 us (87%)
  starting transfers between devices  20.9 us (6%)
  between operations  14.8 us (4%)
  local copies, waits for them, and re-layouts  4.38 us (1%)
    unnamed x2, waiting for transfers between devices  293 us
    all_to_all x1, starting transfers between devices, on_device(): lax.all_to_all(slot_rows, 'sub', split_axis=0, concat_axis=0, tiled=True)  16.9 us
    all_to_all x1, waiting for transfers between devices, on_device(): lax.all_to_all(packed, 'sub', split_axis=0, concat_axis=0, tiled=True)  14.9 us
  transfers between devices with their start and end apart: 3, of which 3 were waited for; matrix products, arithmetic and copies ran while one was open for 2% of the time, Pallas kernels for 0%

commit v1 on v0

v1 whole, which is shorter than its diff:
```python
import functools

import jax
import jax.numpy as jnp
from jax import lax
from jax.experimental import pallas as pl
from jax.experimental.pallas import tpu as pltpu
from jax.sharding import PartitionSpec as P

MESH = pl.DeviceIdType.MESH
BF16, F32, I32 = jnp.bfloat16, jnp.float32, jnp.int32
SLOTS = 2


def kernel(
    dims,
    rows_smem,
    count_smem,
    place_smem,
    factor_hbm,
    tiles_hbm,
    columns_hbm,
    out_ref,
    factor,
    tiles,
    columns,
    parts,
    pack,
    label_out,
    label_in,
    slots_out,
    slots_in,
    pick,
    total,
    sums_out,
    sums_in,
    load_sem,
    label_send,
    label_recv,
    slot_send,
    slot_recv,
    sum_send,
    sum_recv,
    ready,
):
    n_sub, n_blk, n_tiles, cols, rows_here = dims
    n_chip = n_blk // 2
    rows_owned = n_blk * rows_here
    half = n_sub // 2
    sub, blk = lax.axis_index("sub"), lax.axis_index("blk")
    chip, core = blk // 2, blk % 2
    collector = chip * 2 + 1
    barrier = pltpu.get_barrier_semaphore()

    loads = [
        pltpu.make_async_copy(src, dst, load_sem.at[i])
        for i, (src, dst) in enumerate(
            ((columns_hbm, columns), (factor_hbm, factor), (tiles_hbm, tiles))
        )
    ]
    for load in loads:
        load.start()

    @pl.when(core == 1)
    def _():
        def greet_column(i, carry):
            other = lax.rem(sub + i, n_sub)
            pl.semaphore_signal(
                barrier, inc=1, device_id={"sub": other, "blk": collector - 1}, device_id_type=MESH
            )

            @pl.when(i > 0)
            def _():
                pl.semaphore_signal(
                    barrier, inc=1, device_id={"sub": other, "blk": collector}, device_id_type=MESH
                )

            return carry

        lax.fori_loop(0, n_sub, greet_column, 0)

        def greet_plane(i, carry):
            other = lax.rem(chip + i, n_chip) * 2
            for c in range(2):
                pl.semaphore_signal(
                    barrier, inc=1, device_id={"sub": sub, "blk": other + c}, device_id_type=MESH
                )
            return carry

        lax.fori_loop(1, n_chip, greet_plane, 0)

    count = count_smem[0]
    owners, slot_of, local_of = [], [], []
    for t in range(n_tiles):
        row = jnp.clip(rows_smem[0, t], 0, place_smem.shape[0] - 1)
        place = place_smem[row]
        live = t < count
        owner = jnp.where(live, lax.shift_right_logical(place, rows_owned.bit_length() - 1), -1)
        rank = jnp.int32(0)
        for earlier in owners:
            rank = rank + jnp.where(earlier == owner, 1, 0)
        owners.append(owner)
        slot_of.append(jnp.where(live, owner * SLOTS + rank, -1))
        local_of.append(place & (rows_owned - 1))

    width = SLOTS * cols
    per_group = 128 // width
    lane = lax.broadcasted_iota(I32, (n_sub, 128), 1)
    to = lax.broadcasted_iota(I32, (n_sub, 128), 0)
    lane_slot = (lane // cols) % SLOTS
    mine = (lane // width) == lax.rem(sub, per_group)
    label = jnp.zeros((n_sub, 128), I32)
    for t in range(n_tiles):
        hit = mine & (to * SLOTS + lane_slot == slot_of[t])
        label = jnp.where(hit, local_of[t] * cols + lane % cols + 1, label)
    for o in range(n_sub):
        label_out[o] = label[o : o + 1]

    loads[0].wait()
    loads[1].wait()
    projected = lax.dot_general(
        columns[...], factor[...], (((1,), (1,)), ((), ())), preferred_element_type=F32
    ).astype(BF16)
    solved = jnp.dot(projected, factor[...], preferred_element_type=F32).astype(BF16)
    lane1 = lax.broadcasted_iota(I32, (1, 128), 1)
    target = jnp.full((1, 128), -1, I32)
    for t in range(n_tiles):
        at = jnp.where(slot_of[t] >= 0, slot_of[t] * cols, -1024)
        target = jnp.where(lane1 // cols == t, at + lane1 % cols, target)
    row_at = lax.broadcasted_iota(I32, (n_sub * width, 128), 0)
    pack[...] = jnp.where(row_at == target, 1.0, 0.0).astype(BF16)
    loads[2].wait()
    for t in range(n_tiles):
        parts[pl.ds(t * cols, cols)] = jnp.dot(
            solved, tiles[t], preferred_element_type=F32
        ).astype(BF16)
    slots_out[...] = jnp.dot(pack[...], parts[...], preferred_element_type=F32).astype(BF16)

    def slot_copy(dest):
        return pltpu.make_async_remote_copy(
            src_ref=slots_out.at[pl.ds(pl.multiple_of(dest * width, width), width)],
            dst_ref=slots_in.at[core, pl.ds(pl.multiple_of(sub * width, width), width)],
            send_sem=slot_send,
            recv_sem=slot_recv.at[core],
            device_id={"sub": dest, "blk": collector},
            device_id_type=MESH,
        )

    def label_copy(dest):
        return pltpu.make_async_remote_copy(
            src_ref=label_out.at[dest],
            dst_ref=label_in.at[core, sub],
            send_sem=label_send,
            recv_sem=label_recv.at[core],
            device_id={"sub": dest, "blk": collector},
            device_id_type=MESH,
        )

    def dest_of(i):
        k = i // 2
        dz = half // 2 + (1 - 2 * (k % 2)) * ((k + 1) // 2)
        z = lax.rem(sub + dz, half)
        y = (sub // half + 1 + i % 2) % 2
        return y * half + z

    @pl.when(core == 0)
    def _():
        pl.semaphore_wait(barrier, n_sub + n_chip - 1)

        def send(i, carry):
            dest = dest_of(i)
            label_copy(dest).start()
            slot_copy(dest).start()
            return carry

        lax.fori_loop(0, n_sub, send, 0)

        def say_ready(i, carry):
            pl.semaphore_signal(
                ready, inc=1, device_id={"sub": sub, "blk": i * 2 + 1}, device_id_type=MESH
            )
            return carry

        lax.fori_loop(0, n_chip, say_ready, 0)
        pltpu.make_async_copy(label_out, label_out, label_send).wait()
        pltpu.make_async_copy(slots_out, slots_out, slot_send).wait()
        pltpu.make_async_copy(sums_in, sums_in, sum_recv).wait()

    @pl.when(core == 1)
    def _():
        pl.semaphore_wait(barrier, n_sub + n_chip - 2)

        def send(i, carry):
            dest = dest_of(i)
            label_copy(dest).start()
            slot_copy(dest).start()
            return carry

        lax.fori_loop(0, n_sub - 1, send, 0)
        own = pl.ds(pl.multiple_of(sub * width, width), width)
        label_in[1, sub] = label_out[sub]
        slots_in[1, own] = slots_out[own]

        row_in = lax.broadcasted_iota(I32, (rows_owned * cols, 128), 0) + 1

        def add_core(c, sources):
            labels = label_in.at[c, pl.ds(0, sources)]
            pltpu.make_async_copy(labels, labels, label_recv.at[c]).wait()
            for g in range(n_sub // per_group):
                at = label_in[c, g * per_group]
                for s in range(1, per_group):
                    at = at + label_in[c, g * per_group + s]
                pick[:, pl.ds(g * 128, 128)] = jnp.where(row_in == at, 1.0, 0.0).astype(BF16)
            blocks = slots_in.at[c, pl.ds(0, sources * width)]
            pltpu.make_async_copy(blocks, blocks, slot_recv.at[c]).wait()
            return jnp.dot(pick[...], slots_in[c], preferred_element_type=F32)

        total[...] = add_core(1, n_sub - 1)
        sums_out[...] = (total[...] + add_core(0, n_sub)).astype(BF16)

        pl.semaphore_wait(ready, n_chip)
        rows = rows_here * cols

        def sum_copy(dest):
            return pltpu.make_async_remote_copy(
                src_ref=sums_out.at[pl.ds(pl.multiple_of(dest * rows, rows), rows)],
                dst_ref=sums_in.at[chip],
                send_sem=sum_send,
                recv_sem=sum_recv,
                device_id={"sub": sub, "blk": dest},
                device_id_type=MESH,
            )

        def send_sum(i, carry):
            sum_copy(lax.rem(blk + i, n_blk)).start()
            return carry

        lax.fori_loop(1, n_blk, send_sum, 0)
        sums_in[chip] = sums_out[pl.ds(pl.multiple_of(blk * rows, rows), rows)]
        labels = label_out.at[pl.ds(0, n_sub - 1)]
        pltpu.make_async_copy(labels, labels, label_send).wait()
        blocks = slots_out.at[pl.ds(0, (n_sub - 1) * width)]
        pltpu.make_async_copy(blocks, blocks, slot_send).wait()
        sums = sums_out.at[pl.ds(0, (n_blk - 1) * rows)]
        pltpu.make_async_copy(sums, sums, sum_send).wait()
        got = sums_in.at[pl.ds(0, n_chip - 1)]
        pltpu.make_async_copy(got, got, sum_recv).wait()

    acc = sums_in[0].astype(F32)
    for j in range(1, n_chip):
        acc = acc + sums_in[j].astype(F32)
    out_ref[...] = -acc


def on_device(inv_factor, coupling, batch_coupling, tile_rows, tile_count, row_place):
    n_sub, n_blk = lax.axis_size("sub"), lax.axis_size("blk")
    n_tiles, interior, width = coupling.shape[1:]
    cols = batch_coupling.shape[1] * batch_coupling.shape[2]
    rows_here = row_place.shape[0] // (n_sub * n_blk)
    dims = (n_sub, n_blk, n_tiles, cols, rows_here)
    rows_owned = rows_here * n_blk
    slot_rows = n_sub * SLOTS * cols
    smem = pl.BlockSpec(memory_space=pltpu.SMEM)
    hbm = pl.BlockSpec(memory_space=pl.ANY)
    dma = pltpu.SemaphoreType.DMA
    out = pl.pallas_call(
        functools.partial(kernel, dims),
        out_shape=jax.ShapeDtypeStruct((rows_here * cols, width), F32),
        in_specs=[smem, smem, smem, hbm, hbm, hbm],
        out_specs=pl.BlockSpec(memory_space=pltpu.VMEM),
        scratch_shapes=[
            pltpu.VMEM((interior, interior), BF16),
            pltpu.VMEM((n_tiles, interior, width), BF16),
            pltpu.VMEM((cols, interior), BF16),
            pltpu.VMEM((n_tiles * cols, width), BF16),
            pltpu.VMEM((slot_rows, n_tiles * cols), BF16),
            pltpu.VMEM((n_sub, 1, 128), I32),
            pltpu.VMEM((2, n_sub, 1, 128), I32),
            pltpu.VMEM((slot_rows, width), BF16),
            pltpu.VMEM((2, slot_rows, width), BF16),
            pltpu.VMEM((rows_owned * cols, slot_rows), BF16),
            pltpu.VMEM((rows_owned * cols, width), F32),
            pltpu.VMEM((rows_owned * cols, width), BF16),
            pltpu.VMEM((n_blk // 2, rows_here * cols, width), BF16),
            dma((3,)),
            dma,
            dma((2,)),
            dma,
            dma((2,)),
            dma,
            dma,
            pltpu.SemaphoreType.REGULAR,
        ],
        compiler_params=pltpu.CompilerParams(
            collective_id=0, has_side_effects=True, vmem_limit_bytes=24 * 1024 * 1024
        ),
    )(
        tile_rows,
        tile_count,
        row_place,
        inv_factor[0],
        coupling[0],
        batch_coupling.reshape(cols, interior),
    )
    return out.reshape(rows_here, batch_coupling.shape[1], batch_coupling.shape[2], width)


def solution(mesh):
    return jax.shard_map(
        on_device,
        mesh=mesh,
        in_specs=(
            P(("sub", "blk"), None, None),
            P(("sub", "blk"), None, None, None),
            P(("sub", "blk"), None, None, None),
            P(("sub", "blk"), None),
            P(("sub", "blk")),
            P(),
        ),
        out_specs=P(("sub", "blk"), None, None, None),
        check_vma=False,
    )
```

time: 361 us -> 53 us (0.15)
  waiting for transfers between devices: 314 us -> 0 us
  Pallas kernels: 0 us -> 46.3 us
  starting transfers between devices: 20.9 us -> 0 us
  between operations: 14.8 us -> 0.67 us
    unnamed x2 -> x0, waiting for transfers between devices: 293 us -> none
    pallas_call x0 -> x1, Pallas kernels: none -> 46.3 us  [on_device(): pl.pallas_call(functools.partial(kernel, dims), out_shape=jax.ShapeDtypeS...]
    all_to_all x2 -> x0, waiting for transfers between devices: 21 us -> none  [the longest x1 14.9 us: on_device(): lax.all_to_all(packed, 'sub', split_axis=0, concat_axis=0, tiled=True)]
    all_to_all x2 -> x0, starting transfers between devices: 20.9 us -> none  [the longest x1 16.9 us: on_device(): lax.all_to_all(slot_rows, 'sub', split_axis=0, concat_axis=0, tiled=True)]
  transfers between devices with their start and end apart: 3 -> 0, of which waited for: 3 -> 0; matrix products, arithmetic and copies ran while one was open for 2% -> 0% of each run, Pallas kernels for 0% -> 0%
where the time goes in v1:
time: 53 us; the launch traced here: 52.3 us
  Pallas kernels  46.3 us (87%)
  local copies, waits for them, and re-layouts  5.31 us (10%)
  between operations  0.67 us (1%)
    pallas_call x1, Pallas kernels, on_device(): pl.pallas_call(functools.partial(kernel, dims), out_shape=jax.ShapeDtypeS...  46.3 us
    unnamed x11, local copies, waits for them, and re-layouts  5.31 us

profile of v1, /device:TPU:1, one launch (start us, length us, event | category | flops | bytes accessed | tf_op | source)
XLA Modules:
  0.0 52.3 jit_solution(13270136347185728696)
XLA Ops:
  0.7 0.0 copy-start
  0.7 1.6 %copy-done = bf16[1,8,512,256]{3,2,1,0:T(8,128)(2,1)S(1)} copy-done((bf16[1,8,512,256]{3,2,1,0:T(8,128)(2,1)S(1)}, bf16[1,8,512,256]{3,2,1,0:T(8,128)(2,1)}, u32[]{:S(2)}) %copy-start) | copy-done | bytes 2097176
  2.2 0.0 copy-start.1
  2.2 1.0 %copy-done.1 = bf16[1,512,512]{2,1,0:T(8,128)(2,1)S(1)} copy-done((bf16[1,512,512]{2,1,0:T(8,128)(2,1)S(1)}, bf16[1,512,512]{2,1,0:T(8,128)(2,1)}, u32[]{:S(2)}) %copy-start.1) | copy-done | bytes 524312
  3.3 0.0 copy-start.2
  3.3 0.7 %copy-done.2 = bf16[1,1,16,512]{3,2,1,0:T(8,128)(2,1)S(1)} copy-done((bf16[1,1,16,512]{3,2,1,0:T(8,128)(2,1)S(1)}, bf16[1,1,16,512]{3,2,1,0:T(8,128)(2,1)}, u32[]{:S(2)}) %copy-start.2) | copy-done | bytes 16408
  4.0 0.0 copy-start.3
  4.0 0.7 %copy-done.3 = s32[1536]{0:T(1024)S(1)} copy-done((s32[1536]{0:T(1024)S(1)}, s32[1536]{0:T(1024)}, u32[]{:S(2)}) %copy-start.3) | copy-done | bytes 6168
  4.7 0.0 copy-start.4
  4.7 0.7 %copy-done.4 = s32[1,8]{1,0:T(1,128)S(1)} copy-done((s32[1,8]{1,0:T(1,128)S(1)}, s32[1,8]{1,0:T(1,128)}, u32[]{:S(2)}) %copy-start.4) | copy-done | bytes 56
  5.4 46.3 %shard_map.64 = f32[32,256]{1,0:T(8,128)S(1)} custom-call(s32[1,8]{1,0:T(1,128)S(1)} %copy-done.4, s32[1]{0:T(128)S(6)} %copy.9.count_smem, s32[1536]{0:T(1024)S(1)} %copy-done.3, bf16[512,512]{1,0:T(8,128)(2,1)S(1)} %bitcast.7, bf16[8,512,256]{2,1,0:T(8,128)(2,1)S(1)} %bitcast.6, bf16[16,512]{1,0:T(8,128)(2,1)S(1)} %bitcast.9), custom_call_target="tpu_custom_call" | custom-call | tf_op jit(solution)/shard_map/pallas_call | solution.py:266
  51.6 0.6 %copy.10 = f32[2,1,16,256]{3,2,1,0:T(8,128)} copy(f32[2,1,16,256]{3,2,1,0:T(8,128)S(1)} %bitcast.8) | data formatting | bytes 65536
Async XLA Ops:
  0.7 1.6 %copy-start = (bf16[1,8,512,256]{3,2,1,0:T(8,128)(2,1)S(1)}, bf16[1,8,512,256]{3,2,1,0:T(8,128)(2,1)}, u32[]{:S(2)}) copy-start(bf16[1,8,512,256]{3,2,1,0:T(8,128)(2,1)} %param.7) | copy-start | bytes 6291460
  2.2 1.0 %copy-start.1 = (bf16[1,512,512]{2,1,0:T(8,128)(2,1)S(1)}, bf16[1,512,512]{2,1,0:T(8,128)(2,1)}, u32[]{:S(2)}) copy-start(bf16[1,512,512]{2,1,0:T(8,128)(2,1)} %param.6) | copy-start | bytes 1572868
  3.3 0.7 %copy-start.2 = (bf16[1,1,16,512]{3,2,1,0:T(8,128)(2,1)S(1)}, bf16[1,1,16,512]{3,2,1,0:T(8,128)(2,1)}, u32[]{:S(2)}) copy-start(bf16[1,1,16,512]{3,2,1,0:T(8,128)(2,1)} %param.8) | copy-start | bytes 49156
  4.0 0.7 %copy-start.3 = (s32[1536]{0:T(1024)S(1)}, s32[1536]{0:T(1024)}, u32[]{:S(2)}) copy-start(s32[1536]{0:T(1024)} %place_smem.1) | copy-start | bytes 18436
  4.7 0.7 %copy-start.4 = (s32[1,8]{1,0:T(1,128)S(1)}, s32[1,8]{1,0:T(1,128)}, u32[]{:S(2)}) copy-start(s32[1,8]{1,0:T(1,128)} %rows_smem.1) | copy-start | bytes 100

commit v2 on v1

v2 whole, which is shorter than its diff:
```python
import functools

import jax
import jax.numpy as jnp
from jax import lax
from jax.experimental import pallas as pl
from jax.experimental.pallas import tpu as pltpu
from jax.sharding import PartitionSpec as P

MESH = pl.DeviceIdType.MESH
BF16, F32, I32 = jnp.bfloat16, jnp.float32, jnp.int32
SLOTS = 2
LANES = 128


def kernel(
    dims,
    rows_hbm,
    count_hbm,
    place_hbm,
    factor_hbm,
    tiles_hbm,
    columns_hbm,
    out_ref,
    rows_smem,
    count_smem,
    place_smem,
    factor,
    tiles,
    columns,
    parts,
    label_out,
    label_in,
    slots_out,
    slots_in,
    pick,
    sums_out,
    sums_in,
    load_sem,
    label_send,
    label_recv,
    slot_send,
    slot_recv,
    sum_send,
    sum_recv,
):
    n_sub, n_blk, n_tiles, cols, rows_here = dims
    n_chip, n_src, c8 = n_blk // 2, n_sub * 2, cols // 2
    rows_owned = n_blk * rows_here
    half = n_sub // 2
    sub, blk = lax.axis_index("sub"), lax.axis_index("blk")
    chip, core = blk // 2, blk % 2
    barrier = pltpu.get_barrier_semaphore()

    loads = [
        pltpu.make_async_copy(src, dst, load_sem.at[i])
        for i, (src, dst) in enumerate(
            (
                (rows_hbm, rows_smem),
                (count_hbm, count_smem),
                (place_hbm, place_smem),
                (columns_hbm, columns),
                (factor_hbm, factor),
                (tiles_hbm, tiles),
            )
        )
    ]
    for load in loads:
        load.start()

    def greet(dev_sub, dev_blk):
        pl.semaphore_signal(
            barrier, inc=1, device_id={"sub": dev_sub, "blk": dev_blk}, device_id_type=MESH
        )

    def greet_column(i, carry):
        other = lax.rem(sub + i, n_sub)
        greet(other, chip * 2)
        greet(other, chip * 2 + 1)
        return carry

    def greet_plane(i, carry):
        other = lax.rem(chip + i, n_chip) * 2
        greet(sub, other)
        greet(sub, other + 1)
        return carry

    lax.fori_loop(1, n_sub, greet_column, 0)
    greet(sub, blk + 1 - 2 * core)
    lax.fori_loop(1, n_chip, greet_plane, 0)

    for load in loads[:3]:
        load.wait()

    count = count_smem[0]
    owners, slot_of, local_of = [], [], []
    for t in range(n_tiles):
        row = jnp.clip(rows_smem[0, t], 0, place_smem.shape[0] - 1)
        place = place_smem[row]
        live = t < count
        owner = jnp.where(live, lax.shift_right_logical(place, rows_owned.bit_length() - 1), -1)
        rank = jnp.int32(0)
        for earlier in owners:
            rank = rank + jnp.where(earlier == owner, 1, 0)
        owners.append(owner)
        slot_of.append(jnp.where(live, owner * SLOTS + rank, -1024))
        local_of.append(place & (rows_owned - 1))

    width = SLOTS * c8
    per_group = LANES // width
    lane = lax.broadcasted_iota(I32, (n_sub, LANES), 1)
    to = lax.broadcasted_iota(I32, (n_sub, LANES), 0)
    lane_slot = (lane // c8) % SLOTS
    mine = (lane // width) == lax.rem(sub, per_group)
    label = jnp.zeros((n_sub, LANES), I32)
    for t in range(n_tiles):
        hit = mine & (to * SLOTS + lane_slot == slot_of[t])
        label = jnp.where(hit, local_of[t] * c8 + lane % c8 + 1, label)
    for o in range(n_sub):
        label_out[o] = label[o : o + 1]

    loads[3].wait()
    loads[4].wait()
    projected = lax.dot_general(
        columns[...], factor[...], (((1,), (1,)), ((), ())), preferred_element_type=F32
    ).astype(BF16)
    solved = jnp.dot(projected, factor[...], preferred_element_type=F32).astype(BF16)
    in_lane = lax.broadcasted_iota(I32, (1, n_tiles * c8), 1)
    target = jnp.full((1, n_tiles * c8), -1, I32)
    for t in range(n_tiles):
        target = jnp.where(in_lane // c8 == t, slot_of[t] * c8 + in_lane % c8, target)
    row_at = lax.broadcasted_iota(I32, (n_sub * width, n_tiles * c8), 0)
    pack = jnp.where(row_at == target, 1.0, 0.0).astype(BF16)
    loads[5].wait()
    for t in range(0, n_tiles, 2):
        pair = [
            jnp.dot(solved, tiles[u], preferred_element_type=F32) for u in (t, t + 1)
        ]
        for h in range(2):
            for c in range(2):
                cut = [p[c * c8 : (c + 1) * c8, h * LANES : (h + 1) * LANES] for p in pair]
                parts[pl.ds(t * c8, 2 * c8), pl.ds((h * 2 + c) * LANES, LANES)] = (
                    jnp.concatenate(cut, axis=0).astype(BF16)
                )
    for h in range(2):
        slots_out[h] = jnp.dot(
            pack, parts[:, pl.ds(h * 2 * LANES, 2 * LANES)], preferred_element_type=F32
        ).astype(BF16)

    source = core * n_sub + sub

    def slot_copy(dest, h):
        return pltpu.make_async_remote_copy(
            src_ref=slots_out.at[h, pl.ds(pl.multiple_of(dest * width, width), width)],
            dst_ref=slots_in.at[pl.ds(pl.multiple_of(source * width, width), width)],
            send_sem=slot_send,
            recv_sem=slot_recv,
            device_id={"sub": dest, "blk": chip * 2 + h},
            device_id_type=MESH,
        )

    def label_copy(dest, h):
        return pltpu.make_async_remote_copy(
            src_ref=label_out.at[dest],
            dst_ref=label_in.at[source],
            send_sem=label_send,
            recv_sem=label_recv,
            device_id={"sub": dest, "blk": chip * 2 + h},
            device_id_type=MESH,
        )

    def dest_of(i):
        k = i // 2
        dz = half // 2 + (1 - 2 * (k % 2)) * ((k + 1) // 2)
        z = lax.rem(sub + dz, half)
        y = (sub // half + 1 + i % 2) % 2
        return y * half + z

    pl.semaphore_wait(barrier, n_src - 1 + n_blk - 2)
    for h in range(2):

        def send_labels(i, carry, h=h):
            label_copy(dest_of(i), h).start()
            return carry

        def send_slots(i, carry, h=h):
            slot_copy(dest_of(i), h).start()
            return carry

        lax.fori_loop(0, n_sub - 1, send_labels, 0)
        lax.fori_loop(0, n_sub - 1, send_slots, 0)

        @pl.when(core != h)
        def _(h=h):
            label_copy(sub, h).start()
            slot_copy(sub, h).start()

        @pl.when(core == h)
        def _(h=h):
            label_in[source] = label_out[sub]
            slots_in[pl.ds(pl.multiple_of(source * width, width), width)] = slots_out[
                h, pl.ds(pl.multiple_of(sub * width, width), width)
            ]

    labels = label_in.at[pl.ds(0, n_src - 1)]
    pltpu.make_async_copy(labels, labels, label_recv).wait()
    row_in = lax.broadcasted_iota(I32, (rows_owned * c8, LANES), 0) + 1
    for g in range(n_src // per_group):
        at = label_in[g * per_group]
        for s in range(1, per_group):
            at = at + label_in[g * per_group + s]
        pick[:, pl.ds(g * LANES, LANES)] = jnp.where(row_in == at, 1.0, 0.0).astype(BF16)
    blocks = slots_in.at[pl.ds(0, (n_src - 1) * width)]
    pltpu.make_async_copy(blocks, blocks, slot_recv).wait()
    sums_out[...] = jnp.dot(pick[...], slots_in[...], preferred_element_type=F32).astype(BF16)

    rows = rows_here * c8

    def send_sum(i, carry):
        dest = lax.rem(blk + i, n_blk)
        pltpu.make_async_remote_copy(
            src_ref=sums_out.at[pl.ds(pl.multiple_of(dest * rows, rows), rows)],
            dst_ref=sums_in.at[core, chip],
            send_sem=sum_send,
            recv_sem=sum_recv,
            device_id={"sub": sub, "blk": dest},
            device_id_type=MESH,
        ).start()
        return carry

    lax.fori_loop(1, n_blk, send_sum, 0)
    sums_in[core, chip] = sums_out[pl.ds(pl.multiple_of(blk * rows, rows), rows)]
    pltpu.make_async_copy(labels, labels, label_send).wait()
    pltpu.make_async_copy(blocks, blocks, slot_send).wait()
    sums = sums_out.at[pl.ds(0, (n_blk - 1) * rows)]
    pltpu.make_async_copy(sums, sums, sum_send).wait()
    pltpu.make_async_copy(sums, sums, sum_recv).wait()

    for h in range(2):
        acc = sums_in[h, 0].astype(F32)
        for j in range(1, n_chip):
            acc = acc + sums_in[h, j].astype(F32)
        for r in range(rows_here):
            for c in range(2):
                out_ref[pl.ds((r * 2 + c) * c8, c8), pl.ds(h * LANES, LANES)] = -acc[
                    r * c8 : (r + 1) * c8, c * LANES : (c + 1) * LANES
                ]


def on_device(inv_factor, coupling, batch_coupling, tile_rows, tile_count, row_place):
    n_sub, n_blk = lax.axis_size("sub"), lax.axis_size("blk")
    n_tiles, interior, dofs = coupling.shape[1:]
    cols = batch_coupling.shape[1] * batch_coupling.shape[2]
    c8 = cols // 2
    rows_here = row_place.shape[0] // (n_sub * n_blk)
    dims = (n_sub, n_blk, n_tiles, cols, rows_here)
    rows_owned = rows_here * n_blk
    slot_rows = n_sub * SLOTS * c8
    hbm = pl.BlockSpec(memory_space=pltpu.HBM)
    dma = pltpu.SemaphoreType.DMA
    out = pl.pallas_call(
        functools.partial(kernel, dims),
        out_shape=jax.ShapeDtypeStruct((rows_here * cols, dofs), F32),
        in_specs=[hbm] * 6,
        out_specs=pl.BlockSpec(memory_space=pltpu.VMEM),
        scratch_shapes=[
            pltpu.SMEM(tile_rows.shape, I32),
            pltpu.SMEM(tile_count.shape, I32),
            pltpu.SMEM(row_place.shape, I32),
            pltpu.VMEM((interior, interior), BF16),
            pltpu.VMEM((n_tiles, interior, dofs), BF16),
            pltpu.VMEM((cols, interior), BF16),
            pltpu.VMEM((n_tiles * c8, 2 * dofs), BF16),
            pltpu.VMEM((n_sub, 1, LANES), I32),
            pltpu.VMEM((2 * n_sub, 1, LANES), I32),
            pltpu.VMEM((2, slot_rows, dofs), BF16),
            pltpu.VMEM((2 * slot_rows, dofs), BF16),
            pltpu.VMEM((rows_owned * c8, 2 * slot_rows), BF16),
            pltpu.VMEM((rows_owned * c8, dofs), BF16),
            pltpu.VMEM((2, n_blk // 2, rows_here * c8, dofs), BF16),
            dma((6,)),
            dma,
            dma,
            dma,
            dma,
            dma,
            dma,
        ],
        compiler_params=pltpu.CompilerParams(
            collective_id=0, has_side_effects=True, vmem_limit_bytes=60 * 1024 * 1024
        ),
    )(
        tile_rows,
        tile_count,
        row_place,
        inv_factor[0],
        coupling[0],
        batch_coupling.reshape(cols, interior),
    )
    return out.reshape(rows_here, batch_coupling.shape[1], batch_coupling.shape[2], dofs)


def solution(mesh):
    return jax.shard_map(
        on_device,
        mesh=mesh,
        in_specs=(
            P(("sub", "blk"), None, None),
            P(("sub", "blk"), None, None, None),
            P(("sub", "blk"), None, None, None),
            P(("sub", "blk"), None),
            P(("sub", "blk")),
            P(),
        ),
        out_specs=P(("sub", "blk"), None, None, None),
        check_vma=False,
    )
```

time: 53 us -> 46.8 us (0.88)
  local copies, waits for them, and re-layouts: 5.31 us -> 1.38 us
  Pallas kernels: 46.3 us -> 44.6 us
    unnamed x11 -> x1, local copies, waits for them, and re-layouts: 5.31 us -> 1.38 us
    pallas_call x1, Pallas kernels: 46.3 us -> 44.6 us  [on_device(): pl.pallas_call(functools.partial(kernel, dims), out_shape=jax.ShapeDtypeS...]
where the time goes in v2:
time: 46.8 us; the launch traced here: 46.6 us
  Pallas kernels  44.6 us (95%)
  local copies, waits for them, and re-layouts  1.38 us (3%)
  between operations  0.66 us (1%)
    pallas_call x1, Pallas kernels, on_device(): pl.pallas_call(functools.partial(kernel, dims), out_shape=jax.ShapeDtypeS...  44.6 us
    unnamed x1, local copies, waits for them, and re-layouts  1.38 us

profile of v2, /device:TPU:1, one launch (start us, length us, event | category | flops | bytes accessed | tf_op | source)
XLA Modules:
  0.0 46.6 jit_solution(5088014348883929558)
XLA Ops:
  0.7 44.6 %shard_map.64 = f32[32,256]{1,0:T(8,128)} custom-call(s32[1,8]{1,0:T(1,128)} %rows_hbm.1, s32[1]{0:T(128)S(6)} %copy.9.count_hbm, s32[1536]{0:T(1024)} %place_hbm.1, bf16[512,512]{1,0:T(8,128)(2,1)} %bitcast.7, bf16[8,512,256]{2,1,0:T(8,128)(2,1)} %bitcast.6, bf16[16,512]{1,0:T(8,128)(2,1)} %bitcast.9), custom_call_target="tpu_custom_call" | custom-call | tf_op jit(solution)/shard_map/pallas_call | solution.py:261
  45.2 1.4 %copy.10 = f32[2,1,16,256]{3,2,1,0:T(8,128)} copy(f32[2,1,16,256]{3,2,1,0:T(8,128)} %bitcast.8) | data formatting | bytes 65536

commit v3 on v2

--- a/solution.py
+++ b/solution.py
@@ -11,6 +11,9 @@
 BF16, F32, I32 = jnp.bfloat16, jnp.float32, jnp.int32
 SLOTS = 2
 LANES = 128
+LEAD = 24
+PLANE = [(2, x) for x in (2, 1, 3, 0)]
+PLANE += [(y, x) for x in (2, 1, 3, 0) for y in (1, 3)] + [(0, x) for x in (2, 1, 3)]
 
 
 def kernel(
@@ -39,6 +42,8 @@
     load_sem,
     label_send,
     label_recv,
+    pair_send,
+    pair_recv,
     slot_send,
     slot_recv,
     sum_send,
@@ -73,21 +78,23 @@
             barrier, inc=1, device_id={"sub": dev_sub, "blk": dev_blk}, device_id_type=MESH
         )
 
-    def greet_column(i, carry):
-        other = lax.rem(sub + i, n_sub)
+    y, z = sub // half, lax.rem(sub, half)
+    column = []
+    for k in range(half):
+        at = z + half // 2 + (1 - 2 * (k % 2)) * ((k + 1) // 2)
+        at = jnp.where(at >= half, at - half, at)
+        column += [(1 - y) * half + at, y * half + at]
+    plane = []
+    for dy, dx in PLANE:
+        plane.append((((chip // 4 + dy) % 4) * 4 + (chip + dx) % 4) * 2)
+
+    for other in column[:-1]:
         greet(other, chip * 2)
         greet(other, chip * 2 + 1)
-        return carry
-
-    def greet_plane(i, carry):
-        other = lax.rem(chip + i, n_chip) * 2
+    greet(sub, blk + 1 - 2 * core)
+    for other in plane:
         greet(sub, other)
         greet(sub, other + 1)
-        return carry
-
-    lax.fori_loop(1, n_sub, greet_column, 0)
-    greet(sub, blk + 1 - 2 * core)
-    lax.fori_loop(1, n_chip, greet_plane, 0)
 
     for load in loads[:3]:
         load.wait()
@@ -159,51 +166,49 @@
             device_id_type=MESH,
         )
 
-    def label_copy(dest, h):
+    def label_copy(dest):
         return pltpu.make_async_remote_copy(
             src_ref=label_out.at[dest],
             dst_ref=label_in.at[source],
             send_sem=label_send,
             recv_sem=label_recv,
-            device_id={"sub": dest, "blk": chip * 2 + h},
+            device_id={"sub": dest, "blk": blk},
             device_id_type=MESH,
         )
 
-    def dest_of(i):
-        k = i // 2
-        dz = half // 2 + (1 - 2 * (k % 2)) * ((k + 1) // 2)
-        z = lax.rem(sub + dz, half)
-        y = (sub // half + 1 + i % 2) % 2
-        return y * half + z
-
     pl.semaphore_wait(barrier, n_src - 1 + n_blk - 2)
-    for h in range(2):
-
-        def send_labels(i, carry, h=h):
-            label_copy(dest_of(i), h).start()
-            return carry
-
-        def send_slots(i, carry, h=h):
-            slot_copy(dest_of(i), h).start()
-            return carry
-
-        lax.fori_loop(0, n_sub - 1, send_labels, 0)
-        lax.fori_loop(0, n_sub - 1, send_slots, 0)
-
-        @pl.when(core != h)
-        def _(h=h):
-            label_copy(sub, h).start()
-            slot_copy(sub, h).start()
-
-        @pl.when(core == h)
-        def _(h=h):
-            label_in[source] = label_out[sub]
-            slots_in[pl.ds(pl.multiple_of(source * width, width), width)] = slots_out[
-                h, pl.ds(pl.multiple_of(sub * width, width), width)
-            ]
-
-    labels = label_in.at[pl.ds(0, n_src - 1)]
+    for dest in column[:-1]:
+        label_copy(dest).start()
+    label_in[source] = label_out[sub]
+    order = [(k - shift, h, k) for h, shift in ((0, LEAD), (1, 0)) for k in range(n_sub)]
+    for _, h, k in sorted(order):
+        if k < n_sub - 1:
+            slot_copy(column[k], h).start()
+        else:
+
+            @pl.when(core != h)
+            def _(h=h):
+                slot_copy(sub, h).start()
+
+            @pl.when(core == h)
+            def _(h=h):
+                slots_in[pl.ds(pl.multiple_of(source * width, width), width)] = slots_out[
+                    h, pl.ds(pl.multiple_of(sub * width, width), width)
+                ]
+
+    labels = label_in.at[pl.ds(0, n_sub - 1)]
     pltpu.make_async_copy(labels, labels, label_recv).wait()
+    mine = label_in.at[pl.ds(core * n_sub, n_sub)]
+    pair = pltpu.make_async_remote_copy(
+        src_ref=mine,
+        dst_ref=mine,
+        send_sem=pair_send,
+        recv_sem=pair_recv,
+        device_id={"sub": sub, "blk": blk + 1 - 2 * core},
+        device_id_type=MESH,
+    )
+    pair.start()
+    pair.wait_recv()
     row_in = lax.broadcasted_iota(I32, (rows_owned * c8, LANES), 0) + 1
     for g in range(n_src // per_group):
         at = label_in[g * per_group]
@@ -216,27 +221,34 @@
 
     rows = rows_here * c8
 
-    def send_sum(i, carry):
-        dest = lax.rem(blk + i, n_blk)
+    def send_sum(dest):
         pltpu.make_async_remote_copy(
             src_ref=sums_out.at[pl.ds(pl.multiple_of(dest * rows, rows), rows)],
             dst_ref=sums_in.at[core, chip],
             send_sem=sum_send,
-            recv_sem=sum_recv,
+            recv_sem=sum_recv.at[core],
             device_id={"sub": sub, "blk": dest},
             device_id_type=MESH,
         ).start()
-        return carry
-
-    lax.fori_loop(1, n_blk, send_sum, 0)
-    sums_in[core, chip] = sums_out[pl.ds(pl.multiple_of(blk * rows, rows), rows)]
+
+    send_sum(blk + 1 - 2 * core)
+    for other in plane:
+        send_sum(other)
+        send_sum(other + 1)
+    keep = pltpu.make_async_copy(
+        sums_out.at[pl.ds(pl.multiple_of(blk * rows, rows), rows)],
+        sums_in.at[core, chip],
+        sum_recv.at[core],
+    )
+    keep.start()
     pltpu.make_async_copy(labels, labels, label_send).wait()
     pltpu.make_async_copy(blocks, blocks, slot_send).wait()
     sums = sums_out.at[pl.ds(0, (n_blk - 1) * rows)]
     pltpu.make_async_copy(sums, sums, sum_send).wait()
-    pltpu.make_async_copy(sums, sums, sum_recv).wait()
+    pair.wait_send()
 
     for h in range(2):
+        pltpu.make_async_copy(sums_in.at[h], sums_in.at[h], sum_recv.at[h]).wait()
         acc = sums_in[h, 0].astype(F32)
         for j in range(1, n_chip):
             acc = acc + sums_in[h, j].astype(F32)
@@ -285,6 +297,8 @@
             dma,
             dma,
             dma,
+            dma,
+            dma((2,)),
         ],
         compiler_params=pltpu.CompilerParams(
             collective_id=0, has_side_effects=True, vmem_limit_bytes=60 * 1024 * 1024

time: 46.8 us -> 45.5 us (0.972)
  Pallas kernels: 44.6 us -> 43.2 us
    pallas_call x1, Pallas kernels: 44.6 us -> 43.2 us  [on_device(): pl.pallas_call(functools.partial(kernel, dims), out_shape=jax.ShapeDtypeS...]
where the time goes in v3:
time: 45.5 us; the launch traced here: 45.3 us
  Pallas kernels  43.2 us (95%)
  local copies, waits for them, and re-layouts  1.38 us (3%)
  between operations  0.66 us (1%)
    pallas_call x1, Pallas kernels, on_device(): pl.pallas_call(functools.partial(kernel, dims), out_shape=jax.ShapeDtypeS...  43.2 us
    unnamed x1, local copies, waits for them, and re-layouts  1.38 us

profile of v3, /device:TPU:1, one launch (start us, length us, event | category | flops | bytes accessed | tf_op | source)
XLA Modules:
  0.0 45.3 jit_solution(3374098515944838802)
XLA Ops:
  0.7 43.2 %shard_map.64 = f32[32,256]{1,0:T(8,128)} custom-call(s32[1,8]{1,0:T(1,128)} %rows_hbm.1, s32[1]{0:T(128)S(6)} %copy.9.count_hbm, s32[1536]{0:T(1024)} %place_hbm.1, bf16[512,512]{1,0:T(8,128)(2,1)} %bitcast.7, bf16[8,512,256]{2,1,0:T(8,128)(2,1)} %bitcast.6, bf16[16,512]{1,0:T(8,128)(2,1)} %bitcast.9), custom_call_target="tpu_custom_call" | custom-call | tf_op jit(solution)/shard_map/pallas_call | solution.py:273
  43.9 1.4 %copy.10 = f32[2,1,16,256]{3,2,1,0:T(8,128)} copy(f32[2,1,16,256]{3,2,1,0:T(8,128)} %bitcast.8) | data formatting | bytes 65536

commit v4 on v3

--- a/solution.py
+++ b/solution.py
@@ -11,7 +11,6 @@
 BF16, F32, I32 = jnp.bfloat16, jnp.float32, jnp.int32
 SLOTS = 2
 LANES = 128
-LEAD = 24
 PLANE = [(2, x) for x in (2, 1, 3, 0)]
 PLANE += [(y, x) for x in (2, 1, 3, 0) for y in (1, 3)] + [(0, x) for x in (2, 1, 3)]
 
@@ -70,8 +69,6 @@
             )
         )
     ]
-    for load in loads:
-        load.start()
 
     def greet(dev_sub, dev_blk):
         pl.semaphore_signal(
@@ -91,6 +88,8 @@
     for other in column[:-1]:
         greet(other, chip * 2)
         greet(other, chip * 2 + 1)
+    for load in loads:
+        load.start()
     greet(sub, blk + 1 - 2 * core)
     for other in plane:
         greet(sub, other)
@@ -149,10 +148,13 @@
                 parts[pl.ds(t * c8, 2 * c8), pl.ds((h * 2 + c) * LANES, LANES)] = (
                     jnp.concatenate(cut, axis=0).astype(BF16)
                 )
-    for h in range(2):
+
+    def fill_slots(h):
         slots_out[h] = jnp.dot(
             pack, parts[:, pl.ds(h * 2 * LANES, 2 * LANES)], preferred_element_type=F32
         ).astype(BF16)
+
+    fill_slots(0)
 
     source = core * n_sub + sub
 
@@ -180,21 +182,21 @@
     for dest in column[:-1]:
         label_copy(dest).start()
     label_in[source] = label_out[sub]
-    order = [(k - shift, h, k) for h, shift in ((0, LEAD), (1, 0)) for k in range(n_sub)]
-    for _, h, k in sorted(order):
-        if k < n_sub - 1:
-            slot_copy(column[k], h).start()
-        else:
-
-            @pl.when(core != h)
-            def _(h=h):
-                slot_copy(sub, h).start()
-
-            @pl.when(core == h)
-            def _(h=h):
-                slots_in[pl.ds(pl.multiple_of(source * width, width), width)] = slots_out[
-                    h, pl.ds(pl.multiple_of(sub * width, width), width)
-                ]
+    for h in range(2):
+        if h == 1:
+            fill_slots(1)
+        for dest in column[:-1]:
+            slot_copy(dest, h).start()
+
+        @pl.when(core != h)
+        def _(h=h):
+            slot_copy(sub, h).start()
+
+        @pl.when(core == h)
+        def _(h=h):
+            slots_in[pl.ds(pl.multiple_of(source * width, width), width)] = slots_out[
+                h, pl.ds(pl.multiple_of(sub * width, width), width)
+            ]
 
     labels = label_in.at[pl.ds(0, n_sub - 1)]
     pltpu.make_async_copy(labels, labels, label_recv).wait()
@@ -243,8 +245,6 @@
     keep.start()
     pltpu.make_async_copy(labels, labels, label_send).wait()
     pltpu.make_async_copy(blocks, blocks, slot_send).wait()
-    sums = sums_out.at[pl.ds(0, (n_blk - 1) * rows)]
-    pltpu.make_async_copy(sums, sums, sum_send).wait()
     pair.wait_send()
 
     for h in range(2):
@@ -257,6 +257,8 @@
                 out_ref[pl.ds((r * 2 + c) * c8, c8), pl.ds(h * LANES, LANES)] = -acc[
                     r * c8 : (r + 1) * c8, c * LANES : (c + 1) * LANES
                 ]
+    sums = sums_out.at[pl.ds(0, (n_blk - 1) * rows)]
+    pltpu.make_async_copy(sums, sums, sum_send).wait()
 
 
 def on_device(inv_factor, coupling, batch_coupling, tile_rows, tile_count, row_place):

time: 45.5 us -> 45.5 us (level)
  no operation moved by 1% of the time
where the time goes in v4:
time: 45.5 us; the launch traced here: 45.3 us
  Pallas kernels  43.2 us (95%)
  local copies, waits for them, and re-layouts  1.38 us (3%)
  between operations  0.66 us (1%)
    pallas_call x1, Pallas kernels, on_device(): pl.pallas_call(functools.partial(kernel, dims), out_shape=jax.ShapeDtypeS...  43.2 us
    unnamed x1, local copies, waits for them, and re-layouts  1.38 us

profile of v4, /device:TPU:1, one launch (start us, length us, event | category | flops | bytes accessed | tf_op | source)
XLA Modules:
  0.0 45.3 jit_solution(13450824832994654058)
XLA Ops:
  0.7 43.2 %shard_map.64 = f32[32,256]{1,0:T(8,128)} custom-call(s32[1,8]{1,0:T(1,128)} %rows_hbm.1, s32[1]{0:T(128)S(6)} %copy.9.count_hbm, s32[1536]{0:T(1024)} %place_hbm.1, bf16[512,512]{1,0:T(8,128)(2,1)} %bitcast.7, bf16[8,512,256]{2,1,0:T(8,128)(2,1)} %bitcast.6, bf16[16,512]{1,0:T(8,128)(2,1)} %bitcast.9), custom_call_target="tpu_custom_call" | custom-call | tf_op jit(solution)/shard_map/pallas_call | solution.py:275
  43.9 1.4 %copy.10 = f32[2,1,16,256]{3,2,1,0:T(8,128)} copy(f32[2,1,16,256]{3,2,1,0:T(8,128)} %bitcast.8) | data formatting | bytes 65536
